TPU v7x, 32 devices: a whole 2x2x4 slice. The times are simulated.
32 devices in a mesh: space: 8 (over y, x, core), shell: 4 (over z).
Axes of the slice: x: 2, y: 2, z: 4, core: 2. Of those that a mesh axis runs over, the one named last changes fastest.
Arguments:
- weights: float32 [65536], P(('space', 'shell')), may hold values from 0.02 to 1.5
- seg_streamline: int32 [8, 4, 8, 256], P('space', 'shell'), may hold values from 0 to 2047
- seg_features: float32 [8, 4, 8, 256, 128], P('space', 'shell'), may hold values from -12 to 12
- pair_counts: int32 [8, 4, 8], P('space', 'shell'), may hold values from 32 to 256, as said below
- seg_voxel: int32 [8, 4, 8, 256], P('space', 'shell'), may hold values from 0 to 4095
- dictionary: float32 [128, 256], P(None, 'shell'), may hold values from -0.375 to 0.375
- measured: float32 [256, 32768], P('shell', 'space'), may hold values from -6 to 6
Outputs:
- new_weights: float32 [65536], P(('space', 'shell'))
- residual: float32 [256, 32768], P('shell', 'space')
Inputs may be any that keep to these rules, and one draw needn't show every extreme that they name: In each shell group q one voxel block d has pair_counts[s, q, d] = 256 for every s.
All inputs are finite; a program needn't handle non-finite values.
Results may differ from a plain program's by a relative error of at most 0.0003.
Values sent between devices are 32-bit elements; how exact they have to be, the bound alone decides.
A program may use at most 64 MiB of HBM per device.

v0:
```python
import jax
import jax.numpy as jnp
from jax import lax
from jax.sharding import PartitionSpec as P

ITERS = 2


def on_device(weights, seg_streamline, seg_features, pair_counts, seg_voxel, dictionary, measured):
    blocks = seg_streamline.shape[2]
    slots = seg_streamline.shape[3]
    coeffs = seg_features.shape[4]
    voxel_count = measured.shape[1]
    stream_index = seg_streamline.reshape(blocks, slots)
    voxel_index = seg_voxel.reshape(blocks * slots)
    counts = pair_counts.reshape(blocks)
    live_slot = lax.broadcasted_iota(jnp.int32, (blocks, slots), 1) < counts[:, None]
    masked = jnp.where(
        live_slot[:, :, None], seg_features.reshape(blocks, slots, coeffs), jnp.float32(0.0)
    )
    column_sq = (
        jnp.zeros(weights.shape, jnp.float32).at[stream_index].add(jnp.sum(masked * masked, axis=2))
    )
    scaling = 0.5 / (0.5 + column_sq)
    gram_matrix, projected = lax.psum(
        (
            jnp.einsum("jg,kg->jk", dictionary, dictionary, precision=lax.Precision.HIGHEST),
            jnp.einsum("gv,jg->vj", measured, dictionary, precision=lax.Precision.HIGHEST),
        ),
        "shell",
    )
    current = weights
    residual = jnp.zeros(measured.shape, jnp.float32)
    for iteration in range(ITERS):
        picked = current[stream_index]
        seg_terms = lax.all_to_all(
            picked[:, :, None] * masked, "space", split_axis=0, concat_axis=0, tiled=True
        )
        partial_coeff = (
            jnp.zeros((voxel_count, coeffs), jnp.float32)
            .at[voxel_index]
            .add(seg_terms.reshape(blocks * slots, coeffs))
        )
        coeff_sum = lax.psum(partial_coeff, "shell")
        residual = (
            jnp.einsum("jg,vj->gv", dictionary, coeff_sum, precision=lax.Precision.HIGHEST)
            - measured
        )
        adjoint = jnp.dot(coeff_sum, gram_matrix, precision=lax.Precision.HIGHEST) - projected
        adj_rows = adjoint[voxel_index].reshape(blocks, slots, coeffs)
        grad_slot = jnp.sum(
            masked * lax.all_to_all(adj_rows, "space", split_axis=0, concat_axis=0, tiled=True),
            axis=2,
        )
        gradient = jnp.zeros(weights.shape, jnp.float32).at[stream_index].add(grad_slot)
        current = jnp.maximum(current - scaling * gradient, 0.0)
    return (current, residual)


def solution(mesh):
    in_specs = (
        P(("space", "shell")),
        P("space", "shell", None, None),
        P("space", "shell", None, None, None),
        P("space", "shell", None),
        P("space", "shell", None, None),
        P(None, "shell"),
        P("shell", "space"),
    )
    out_specs = (P(("space", "shell")), P("shell", "space"))
    return jax.shard_map(
        on_device, mesh=mesh, in_specs=in_specs, out_specs=out_specs, check_vma=False
    )
```

profile of v0, /device:TPU:0, one launch (start us, length us, event | category | flops | bytes accessed | tf_op | source)
XLA Modules:
  0.0 446.1 jit_solution(8587018203023521038)
XLA Ops:
  7.2 0.7 fusion.7
  7.9 11.8 %gather_fusion = f32[2048]{0:T(1024)S(1)} fusion(f32[2048]{0:T(1024)S(1)} %copy-done.1, s32[2048]{0:T(1024)S(1)} %broadcast_clamp_fusion.1), kind=kCustom, calls=%fused_computation | custom fusion | bytes 24576 | tf_op jit(solution)/shard_map/gather | solution.py:35
  19.8 0.1 iota_compare_fusion
  19.8 1.5 fusion.6
  21.3 5.2 %all-to-all-start = ((f32[8,256,128]{2,1,0:T(8,128)}), f32[8,256,128]{2,1,0:T(8,128)S(1)}, u32[]{:S(2)}, u32[]{:S(2)}) async-start(f32[8,256,128]{2,1,0:T(8,128)} %fusion.6), calls=%async_computation | async-start | bytes 2097152 | tf_op jit(solution)/shard_map/all_to_all | solution.py:36
  26.5 0.0 all-reduce.6.cloned.1.call-start
  26.6 0.9 fusion.14
  27.5 4.8 %fusion.15 = f32[4096,128]{1,0:T(8,128)} fusion(f32[64,4096]{1,0:T(8,128)S(1)} %copy-done.4, f32[128,64]{0,1:T(8,128)S(1)} %copy-done), kind=kOutput, calls=%fused_computation.39 | convolution fusion | flops 402653184 | bytes 3178496 | tf_op jit(solution)/shard_map/gv,jg->vj/dot_general | solution.py:28
  32.3 9.6 %all-to-all-done = f32[8,256,128]{2,1,0:T(8,128)S(1)} async-done(((f32[8,256,128]{2,1,0:T(8,128)}), f32[8,256,128]{2,1,0:T(8,128)S(1)}, u32[]{:S(2)}, u32[]{:S(2)}) %all-to-all-start) | async-done | bytes 1048608 | tf_op jit(solution)/shard_map/all_to_all | solution.py:36
  41.9 12.9 %scatter_custom_fusion.1 = f32[4096,128]{1,0:T(8,128)} fusion(s32[2048]{0:T(1024)S(1)} %bitcast.59, f32[2048,128]{1,0:T(8,128)S(1)} %bitcast.50, f32[]{:T(128)} %constant.0.clone.1), kind=kCustom, calls=%fused_computation.18 | custom fusion | flops 262144 | bytes 2097156 | tf_op jit(solution)/shard_map/scatter-add | solution.py:42
  54.8 0.0 all-reduce.6.cloned.1.call-update
  54.8 0.0 all-reduce.4.cloned.1.call-start
  54.9 157.3 %all-reduce.6.cloned.1.call-done = (f32[4096,128]{1,0:T(8,128)}, f32[4096,128]{1,0:T(8,128)}, f32[128,128]{1,0:T(8,128)}) async-done(((f32[4096,128]{1,0:T(8,128)}, f32[4096,128]{1,0:T(8,128)}, f32[128,128]{1,0:T(8,128)}), (f32[4096,128]{1,0:T(8,128)}, f32[4096,128]{1,0:T(8,128)}, f32[128,128]{1,0:T(8,128)})) %all-reduce.6.cloned.1.call-update) | async-done | bytes 4259856 | tf_op jit(solution)/shard_map/psum | solution.py:25
  212.2 4.1 convolution_subtract_fusion.1
  216.3 7.6 %gather_fusion.1 = f32[2048,128]{1,0:T(8,128)} fusion(f32[4096,128]{1,0:T(8,128)S(1)} %convolution_subtract_fusion.1, s32[2048]{0:T(1024)S(1)} %broadcast_clamp_fusion), kind=kCustom, calls=%fused_computation.1 | custom fusion | bytes 2105344 | tf_op jit(solution)/shard_map/gather | solution.py:50
  224.0 19.0 %all_to_all.20 = f32[8,256,128]{2,1,0:T(8,128)S(1)} all-to-all(f32[8,256,128]{2,1,0:T(8,128)} %bitcast.49), channel_id=1, replica_groups=mesh['space'=8,'shell'=4] {'space'}, dimensions={0} | all-to-all | bytes 2097152 | tf_op jit(solution)/shard_map/all_to_all | solution.py:52
  243.0 1.0 multiply_reduce_fusion.2
  244.0 11.3 %scatter_custom_fusion.2 = f32[2048]{0:T(1024)S(1)} fusion(s32[2048]{0:T(1024)S(1)} %bitcast.56, f32[2048]{0:T(1024)S(1)} %bitcast.65, f32[]{:T(128)} %constant.0.clone.1), kind=kCustom, calls=%fused_computation.33 | custom fusion | flops 2048 | bytes 8196 | tf_op jit(solution)/shard_map/scatter-add | solution.py:55
  255.4 11.5 %scatter_custom_fusion = f32[2048]{0:T(1024)S(1)} fusion(s32[2048]{0:T(1024)S(1)} %bitcast.57, f32[2048]{0:T(1024)S(1)} %bitcast.63, f32[]{:T(128)} %constant.5.clone.1), kind=kCustom, calls=%fused_computation.36 | custom fusion | flops 2048 | bytes 8196 | tf_op jit(solution)/shard_map/scatter-add | solution.py:22
  267.0 11.8 %gather_fusion.2 = f32[2048]{0:T(1024)S(1)} fusion(f32[2048]{0:T(1024)S(1)} %subtract_maximum_fusion.1, s32[2048]{0:T(1024)S(1)} %broadcast_clamp_fusion.1), kind=kCustom, calls=%fused_computation.2 | custom fusion | bytes 24576 | tf_op jit(solution)/shard_map/gather | solution.py:35
  278.8 0.7 fusion.5
  279.5 17.8 %all_to_all.21 = f32[8,256,128]{2,1,0:T(8,128)S(1)} all-to-all(f32[8,256,128]{2,1,0:T(8,128)S(1)} %fusion.5), channel_id=1, replica_groups=mesh['space'=8,'shell'=4] {'space'}, dimensions={0} | all-to-all | bytes 2097152 | tf_op jit(solution)/shard_map/all_to_all | solution.py:36
  297.3 12.9 %scatter_custom_fusion.3 = f32[4096,128]{1,0:T(8,128)} fusion(s32[2048]{0:T(1024)S(1)} %bitcast.61, f32[2048,128]{1,0:T(8,128)S(1)} %bitcast.51, f32[]{:T(128)} %constant.0.clone.1), kind=kCustom, calls=%fused_computation.16 | custom fusion | flops 262144 | bytes 2097156 | tf_op jit(solution)/shard_map/scatter-add | solution.py:42
  310.2 83.9 %all-reduce.4.cloned.1.call-done = f32[4096,128]{1,0:T(8,128)} async-done(((f32[4096,128]{1,0:T(8,128)}), f32[4096,128]{1,0:T(8,128)}) %all-reduce.4.cloned.1.call-update) | async-done | bytes 2097168 | tf_op jit(solution)/shard_map/psum | solution.py:44
  394.0 4.0 convolution_subtract_fusion
  398.0 7.6 %gather_fusion.3 = f32[2048,128]{1,0:T(8,128)} fusion(f32[4096,128]{1,0:T(8,128)S(1)} %convolution_subtract_fusion, s32[2048]{0:T(1024)S(1)} %broadcast_clamp_fusion), kind=kCustom, calls=%fused_computation.3 | custom fusion | bytes 2105344 | tf_op jit(solution)/shard_map/gather | solution.py:50
  405.6 4.4 all-to-all-start.3
  410.0 4.6 %fusion = f32[64,4096]{1,0:T(8,128)} fusion(f32[64,4096]{1,0:T(8,128)} %param.13, f32[4096,128]{1,0:T(8,128)S(1)} %copy-done.3, f32[128,64]{0,1:T(8,128)S(1)} %copy-done), kind=kOutput, calls=%fused_computation.12 | convolution fusion | flops 402915328 | bytes 4227072 | tf_op jit(solution)/shard_map/jg,vj->gv/dot_general | solution.py:46
  414.6 10.8 %all-to-all-done.3 = f32[8,256,128]{2,1,0:T(8,128)} async-done(((f32[8,256,128]{2,1,0:T(8,128)}), f32[8,256,128]{2,1,0:T(8,128)}, u32[]{:S(2)}, u32[]{:S(2)}) %all-to-all-start.3) | async-done | bytes 1048608 | tf_op jit(solution)/shard_map/all_to_all | solution.py:52
  425.4 1.9 multiply_reduce_fusion
  427.3 11.3 %scatter_custom_fusion.4 = f32[2048]{0:T(1024)S(1)} fusion(s32[2048]{0:T(1024)S(1)} %bitcast.58, f32[2048]{0:T(1024)S(1)} %bitcast.64, f32[]{:T(128)} %constant.0.clone.1), kind=kCustom, calls=%fused_computation.31 | custom fusion | flops 2048 | bytes 8196 | tf_op jit(solution)/shard_map/scatter-add | solution.py:55
  438.6 0.6 subtract_maximum_fusion
  (28 shorter events, 0.1 us)
Async XLA Ops:
  7.2 19.4 %copy-start = (f32[128,64]{0,1:T(8,128)S(1)}, f32[128,64]{0,1:T(8,128)}, u32[]{:S(2)}) copy-start(f32[128,64]{0,1:T(8,128)} %param.12) | copy-start | bytes 98308
  7.2 0.7 copy-start.1
  7.9 11.8 %copy-start.7 = (s32[1,1,8]{2,1,0:T(1,128)S(1)}, s32[1,1,8]{2,1,0:T(1,128)}, u32[]{:S(2)}) copy-start(s32[1,1,8]{2,1,0:T(1,128)} %param.10) | copy-start | bytes 100
  7.9 11.9 %copy-start.2 = (f32[1,1,8,256,128]{4,3,2,1,0:T(8,128)S(1)}, f32[1,1,8,256,128]{4,3,2,1,0:T(8,128)}, u32[]{:S(2)}) copy-start(f32[1,1,8,256,128]{4,3,2,1,0:T(8,128)} %param.9) | copy-start | bytes 3145732
  19.8 6.7 %copy-start.6 = (s32[1,1,8,256]{3,2,1,0:T(8,128)S(1)}, s32[1,1,8,256]{3,2,1,0:T(8,128)}, u32[]{:S(2)}) copy-start(s32[1,1,8,256]{3,2,1,0:T(8,128)} %param.11) | copy-start | bytes 24580
  19.8 7.7 %copy-start.4 = (f32[64,4096]{1,0:T(8,128)S(1)}, f32[64,4096]{1,0:T(8,128)}, u32[]{:S(2)}) copy-start(f32[64,4096]{1,0:T(8,128)} %param.13) | copy-start | bytes 3145732
  21.3 20.6 %all-to-all-start = ((f32[8,256,128]{2,1,0:T(8,128)}), f32[8,256,128]{2,1,0:T(8,128)S(1)}, u32[]{:S(2)}, u32[]{:S(2)}) async-start(f32[8,256,128]{2,1,0:T(8,128)} %fusion.6), calls=%async_computation | async-start | bytes 2097152 | tf_op jit(solution)/shard_map/all_to_all | solution.py:36
  26.5 185.7 %all-reduce.6.cloned.1.call-start = ((), (), s32[]{:S(2)}) async-start(), calls=%async_computation.5 | async-start | bytes 8519680 | tf_op jit(solution)/shard_map/psum | solution.py:25
  54.8 339.2 %all-reduce.4.cloned.1.call-start = ((), (), s32[]{:S(2)}) async-start(), calls=%async_computation.4 | async-start | bytes 4194304 | tf_op jit(solution)/shard_map/psum | solution.py:44
  297.3 96.8 %copy-start.5 = (f32[128,128]{1,0:T(8,128)S(1)}, f32[128,128]{1,0:T(8,128)}, u32[]{:S(2)}) copy-start(f32[128,128]{1,0:T(8,128)} %get-tuple-element.6) | copy-start | bytes 196612
  405.6 4.4 copy-start.3
  405.6 19.8 %all-to-all-start.3 = ((f32[8,256,128]{2,1,0:T(8,128)}), f32[8,256,128]{2,1,0:T(8,128)}, u32[]{:S(2)}, u32[]{:S(2)}) async-start(f32[8,256,128]{2,1,0:T(8,128)} %bitcast.48), calls=%async_computation.3 | async-start | bytes 2097152 | tf_op jit(solution)/shard_map/all_to_all | solution.py:52
Sparse Core Ops, SparseCore 0:
  55.0 157.2 all-reduce.5
  310.3 83.6 all-reduce.3
where the time goes:
time: 447 us; the launch traced here: 446 us
  waiting for transfers between devices  262 us (59%)
  other arithmetic  66.5 us (15%)
  local copies, waits for them, and re-layouts  38.9 us (9%)
  blocking collectives  36.8 us (8%)
  matrix products  18.4 us (4%)
  between operations  14.3 us (3%)
  starting transfers between devices  9.61 us (2%)
    psum x1, waiting for transfers between devices, on_device(): lax.psum((jnp.einsum('jg,kg->jk', dictionary, dictionary, precision=lax.P...  157 us
    psum x1, waiting for transfers between devices, on_device(): coeff_sum = lax.psum(partial_coeff, 'shell')  83.9 us
    scatter-add x2, other arithmetic, on_device(): partial_coeff = jnp.zeros((voxel_count, coeffs), jnp.float32).at[voxel_in...  25.8 us
    gather x4, local copies, waits for them, and re-layouts, on_device(): picked = current[stream_index]  23.6 us
    scatter-add x2, other arithmetic, on_device(): jnp.zeros(weights.shape, jnp.float32).at[stream_index].add(grad_slot)  22.7 us
    all_to_all x1, blocking collectives, on_device(): lax.all_to_all(adj_rows, 'space', split_axis=0, concat_axis=0, tiled=True)  19 us
    all_to_all x1, blocking collectives, on_device(): lax.all_to_all(picked[:, :, None] * masked, 'space', split_axis=0, concat...  17.8 us
    gather x2, local copies, waits for them, and re-layouts, on_device(): adj_rows = adjoint[voxel_index].reshape(blocks, slots, coeffs)  15.2 us
  transfers between devices with their start and end apart: 4, of which 4 were waited for; matrix products, arithmetic and copies ran while one was open for 2% of the time, Pallas kernels for 0%

commit v1 on v0

v1 whole, which is shorter than its diff:
```python
import functools

import jax
import jax.numpy as jnp
from jax import lax
from jax.experimental import pallas as pl
from jax.experimental.pallas import tpu as pltpu
from jax.sharding import PartitionSpec as P

ITERS = 2
LANES = 128
ROWS_STEP = 8
HIGH = lax.Precision.HIGHEST


def local_kernel(dirs, voxel_ref, x_ref, counts_ref, pairs_ref, start_ref, resid_ref, grad_ref,
                 even0, odd0, even1, odd1, products):
    blocks = counts_ref.shape[0]
    rows = pairs_ref.shape[0] // blocks
    even0[...] = start_ref[...]
    odd0[...] = jnp.zeros_like(odd0)
    even1[...] = jnp.zeros_like(even1)
    odd1[...] = jnp.zeros_like(odd1)
    products[...] = jnp.zeros_like(products)

    def steps_of(block):
        return lax.div(counts_ref[block] + (2 * ROWS_STEP - 1), 2 * ROWS_STEP)

    def scatter_block(block, carry):
        def step(at, carry):
            base = pl.multiple_of(block * rows + at * ROWS_STEP, ROWS_STEP)
            scal = block * (2 * rows) + at * ROWS_STEP
            tile = pairs_ref[pl.ds(base, ROWS_STEP), :]
            for r in range(ROWS_STEP):
                row = tile[r:r + 1, :]
                even, odd = (even0, odd0) if r % 2 == 0 else (even1, odd1)
                va = voxel_ref[scal + r]
                vb = voxel_ref[scal + rows + r]
                even[pl.ds(va, 1), :] = even[pl.ds(va, 1), :] + x_ref[scal + r] * row
                odd[pl.ds(vb, 1), :] = odd[pl.ds(vb, 1), :] + x_ref[scal + rows + r] * row
            return carry

        return lax.fori_loop(0, steps_of(block), step, carry)

    lax.fori_loop(0, blocks, scatter_block, 0)

    left = lax.broadcasted_iota(jnp.int32, (LANES, 2 * dirs), 1) < dirs

    def combine(at, carry):
        part = pl.ds(pl.multiple_of(at * LANES, LANES), LANES)
        both = jnp.where(left, even0[part, :] + even1[part, :], odd0[part, :] + odd1[part, :])
        resid_ref[part, :] = both + pltpu.roll(both, dirs, 1)
        return carry

    lax.fori_loop(0, resid_ref.shape[0] // LANES, combine, 0)

    left_row = lax.broadcasted_iota(jnp.int32, (1, 2 * dirs), 1) < dirs

    def gather_block(block, carry):
        def step(at, carry):
            base = pl.multiple_of(block * rows + at * ROWS_STEP, ROWS_STEP)
            scal = block * (2 * rows) + at * ROWS_STEP
            picked = []
            for r in range(ROWS_STEP):
                va = voxel_ref[scal + r]
                vb = voxel_ref[scal + rows + r]
                picked.append(
                    jnp.where(left_row, resid_ref[pl.ds(va, 1), :], resid_ref[pl.ds(vb, 1), :])
                )
            tile = jnp.concatenate(picked, axis=0)
            products[pl.ds(base, ROWS_STEP), :] = tile * pairs_ref[pl.ds(base, ROWS_STEP), :]
            return carry

        return lax.fori_loop(0, steps_of(block), step, carry)

    lax.fori_loop(0, blocks, gather_block, 0)

    half = lax.broadcasted_iota(jnp.int32, (8, 2 * dirs), 0)
    lane = lax.broadcasted_iota(jnp.int32, (8, 2 * dirs), 1)
    select = jnp.where(lax.div(lane, dirs) == half, 1.0, 0.0).astype(jnp.float32)

    def reduce_rows(block, carry):
        part = products[pl.ds(pl.multiple_of(block * rows, rows), rows), :]
        sums = lax.dot_general(
            select, part, (((1,), (1,)), ((), ())), precision=HIGH,
            preferred_element_type=jnp.float32,
        )
        grad_ref[block] = sums[0:2, :]
        return carry

    lax.fori_loop(0, blocks, reduce_rows, 0)


def local_step(voxel, x_slots, counts, pairs, start, dirs):
    blocks = counts.shape[0]
    rows = pairs.shape[0] // blocks
    voxels = start.shape[0]
    vmem = pl.BlockSpec(memory_space=pltpu.VMEM)
    smem = pl.BlockSpec(memory_space=pltpu.SMEM)
    wide = pltpu.VMEM((voxels, 2 * dirs), jnp.float32)
    return pl.pallas_call(
        functools.partial(local_kernel, dirs),
        out_shape=(
            jax.ShapeDtypeStruct((voxels, 2 * dirs), jnp.float32),
            jax.ShapeDtypeStruct((blocks, 2, rows), jnp.float32),
        ),
        in_specs=[smem, smem, smem, vmem, vmem],
        out_specs=(vmem, vmem),
        scratch_shapes=[wide, wide, wide, wide, pltpu.VMEM(pairs.shape, jnp.float32)],
        compiler_params=pltpu.CompilerParams(vmem_limit_bytes=56 * 1024 * 1024),
        cost_estimate=pl.CostEstimate(flops=10**8, bytes_accessed=10**8, transcendentals=0),
    )(voxel, x_slots, counts, pairs, start)


def on_device(shells, weights, seg_streamline, seg_features, pair_counts, seg_voxel, dictionary,
              measured):
    blocks = seg_streamline.shape[2]
    slots = seg_streamline.shape[3]
    coeffs = seg_features.shape[4]
    rows = slots // 2
    dirs = dictionary.shape[1]
    streams = weights.shape[0]
    counts = pair_counts.reshape(blocks)

    owner = seg_streamline.reshape(blocks, rows, 2).transpose(0, 2, 1).reshape(-1)
    voxel = seg_voxel.reshape(blocks, rows, 2).transpose(0, 2, 1).reshape(blocks, slots)
    voxel_all = (
        lax.all_gather(voxel, "shell", axis=0).transpose(1, 0, 2).reshape(blocks * shells * slots)
    )
    dict_all = lax.all_gather(dictionary, "shell", axis=0)

    live = lax.broadcasted_iota(jnp.int32, (blocks, slots), 1) < counts[:, None]
    masked = jnp.where(
        live[:, :, None], seg_features.reshape(blocks, slots, coeffs), jnp.float32(0.0)
    )
    feat_pairs = masked.reshape(blocks * rows, 2 * coeffs)
    sq = jnp.sum((masked * masked).reshape(blocks, rows, 2, coeffs), axis=3)
    sq = sq.transpose(0, 2, 1).reshape(-1)

    hi = (owner // LANES)[:, None] == lax.broadcasted_iota(jnp.int32, (1, streams // LANES), 1)
    lo = (owner % LANES)[:, None] == lax.broadcasted_iota(jnp.int32, (1, LANES), 1)
    hi = hi.astype(jnp.float32)

    def pick(table):
        wide = jnp.dot(hi, table, precision=HIGH)
        return jnp.sum(jnp.where(lo, wide, 0.0), axis=1)

    def add_up(values):
        return lax.dot_general(
            hi, jnp.where(lo, values[:, None], 0.0), (((0,), (0,)), ((), ())), precision=HIGH
        )

    scaling = 0.5 / (0.5 + add_up(sq))

    zero = jnp.zeros_like(dict_all)
    weave = jnp.stack(
        [jnp.concatenate([dict_all, zero], axis=2), jnp.concatenate([zero, dict_all], axis=2)],
        axis=1,
    ).reshape(shells, 2 * coeffs, 2 * dirs)
    projected = jnp.einsum("rk,qkc->qrc", feat_pairs, weave, precision=HIGH)
    projected = projected.reshape(shells, blocks, rows, 2 * dirs).transpose(1, 0, 2, 3)
    pairs = lax.all_to_all(
        projected.reshape(blocks * shells, rows, 2 * dirs), ("space", "shell"), 0, 0, tiled=True
    ).reshape(blocks * shells * rows, 2 * dirs)

    start = jnp.concatenate([-measured.T, jnp.zeros_like(measured).T], axis=1)

    current = weights.reshape(streams // LANES, LANES)
    counts_all = None
    for iteration in range(ITERS):
        sent = pick(current).reshape(blocks, slots)
        if iteration == 0:
            extra = jnp.broadcast_to(counts[:, None].astype(jnp.float32), (blocks, LANES))
            sent = jnp.concatenate([sent, extra], axis=1)
        sent = jnp.broadcast_to(sent[:, None, :], (blocks, shells, sent.shape[1]))
        got = lax.all_to_all(
            sent.reshape(blocks * shells, -1), ("space", "shell"), 0, 0, tiled=True
        )
        if iteration == 0:
            counts_all = got[:, slots].astype(jnp.int32)
        resid, grads = local_step(
            voxel_all, got[:, :slots].reshape(-1), counts_all, pairs, start, dirs
        )
        back = lax.all_to_all(
            grads.reshape(blocks * shells, slots), ("space", "shell"), 0, 0, tiled=True
        )
        slot_grad = jnp.sum(back.reshape(blocks, shells, slots), axis=1)
        current = jnp.maximum(current - scaling * add_up(slot_grad.reshape(-1)), 0.0)
    return current.reshape(streams), resid[:, :dirs].T


def solution(mesh):
    in_specs = (
        P(("space", "shell")),
        P("space", "shell", None, None),
        P("space", "shell", None, None, None),
        P("space", "shell", None),
        P("space", "shell", None, None),
        P(None, "shell"),
        P("shell", "space"),
    )
    out_specs = (P(("space", "shell")), P("shell", "space"))
    return jax.shard_map(
        functools.partial(on_device, mesh.shape["shell"]),
        mesh=mesh, in_specs=in_specs, out_specs=out_specs, check_vma=False,
    )
```

time: 447 us -> 196 us (0.44)
  waiting for transfers between devices: 262 us -> 10.2 us
  other arithmetic: 66.5 us -> 5.01 us
  Pallas kernels: 0 us -> 44.9 us
  blocking collectives: 36.8 us -> 76.7 us
  starting transfers between devices: 9.61 us -> 32.3 us
  local copies, waits for them, and re-layouts: 38.9 us -> 16.9 us
  between operations: 14.3 us -> 0.89 us
  matrix products: 18.4 us -> 10 us
    psum x2 -> x0, waiting for transfers between devices: 241 us -> none  [the longest x1 157 us: on_device(): lax.psum((jnp.einsum('jg,kg->jk', dictionary, dictionary, precision=lax.P...]
    all_gather x0 -> x2, blocking collectives: none -> 67.1 us  [the longest x1 53.2 us: on_device(): lax.all_gather(voxel, 'shell', axis=0).transpose(1, 0, 2)]
    scatter-add x5 -> x0, other arithmetic: 60 us -> none  [the longest x2 25.8 us: on_device(): partial_coeff = jnp.zeros((voxel_count, coeffs), jnp.float32).at[voxel_in...]
    pallas_call x0 -> x2, Pallas kernels: none -> 44.9 us  [local_step(): pl.pallas_call(functools.partial(local_kernel, dirs), out_shape=(jax.Shap...]
    gather x6 -> x0, local copies, waits for them, and re-layouts: 38.8 us -> none  [the longest x4 23.6 us: on_device(): picked = current[stream_index]]
    all_to_all x2 -> x1, blocking collectives: 36.8 us -> 9.61 us  [on_device(): lax.all_to_all(sent.reshape(blocks * shells, -1), ('space', 'shell'), 0,...]
    all_to_all x2 -> x4, starting transfers between devices: 9.53 us -> 32.3 us  [the longest x2 19.5 us: on_device(): lax.all_to_all(grads.reshape(blocks * shells, slots), ('space', 'shell'),...]
    all_to_all x2 -> x4, waiting for transfers between devices: 20.4 us -> 10.2 us  [the longest x2 10.2 us: on_device(): lax.all_to_all(grads.reshape(blocks * shells, slots), ('space', 'shell'),...]
  transfers between devices with their start and end apart: 4 -> 4, of which waited for: 4 -> 2; matrix products, arithmetic and copies ran while one was open for 2% -> 11% of each run, Pallas kernels for 0% -> 0%
where the time goes in v1:
time: 196 us; the launch traced here: 197 us
  blocking collectives  76.7 us (39%)
  Pallas kernels  44.9 us (23%)
  starting transfers between devices  32.3 us (16%)
  local copies, waits for them, and re-layouts  16.9 us (9%)
  waiting for transfers between devices  10.2 us (5%)
  matrix products  10 us (5%)
  other arithmetic  5.01 us (3%)
    all_gather x1, blocking collectives, on_device(): lax.all_gather(voxel, 'shell', axis=0).transpose(1, 0, 2)  53.2 us
    pallas_call x2, Pallas kernels, local_step(): pl.pallas_call(functools.partial(local_kernel, dirs), out_shape=(jax.Shap...  44.9 us
    all_to_all x2, starting transfers between devices, on_device(): lax.all_to_all(grads.reshape(blocks * shells, slots), ('space', 'shell'),...  19.5 us
    all_gather x1, blocking collectives, on_device(): dict_all = lax.all_gather(dictionary, 'shell', axis=0)  14 us
    all_to_all x2, waiting for transfers between devices, on_device(): lax.all_to_all(grads.reshape(blocks * shells, slots), ('space', 'shell'),...  10.2 us
    all_to_all x1, blocking collectives, on_device(): lax.all_to_all(sent.reshape(blocks * shells, -1), ('space', 'shell'), 0,...  9.61 us
    all_to_all x1, starting transfers between devices, on_device(): lax.all_to_all(sent.reshape(blocks * shells, -1), ('space', 'shell'), 0,...  7.3 us
    unnamed x18, local copies, waits for them, and re-layouts  5.57 us
  transfers between devices with their start and end apart: 4, of which 2 were waited for; matrix products, arithmetic and copies ran while one was open for 11% of the time, Pallas kernels for 0%

profile of v1, /device:TPU:0, one launch (start us, length us, event | category | flops | bytes accessed | tf_op | source)
XLA Modules:
  0.0 197.0 jit_solution(18100894695378549889)
XLA Ops:
  0.6 0.7 bitcast_convert_fusion
  1.3 0.8 copy.51
  2.2 2.0 %fusion = f32[2048]{0:T(1024)S(1)} fusion(s32[2048]{0:T(1024)S(1)} %get-tuple-element.21, s32[2048]{0:T(1024)S(1)} %get-tuple-element.20, f32[2048]{0:T(1024)} %param.7), kind=kOutput, calls=%fused_computation.3 | convolution fusion | flops 51148800 | bytes 32768 | tf_op jit(solution)/shard_map/dot_general | solution.py:145
  4.3 0.7 all_to_all.39
  5.0 7.3 %all-to-all-start = ((f32[32,1,384]{2,1,0:T(1,128)}), f32[32,1,384]{2,1,0:T(1,128)S(1)}, u32[]{:S(2)}, u32[]{:S(2)}) async-start(f32[32,1,384]{2,1,0:T(1,128)} %all_to_all.39), calls=%async_computation | async-start | bytes 98304 | tf_op jit(solution)/shard_map/all_to_all | solution.py:176
  12.3 0.7 iota_compare_fusion.7
  13.0 14.0 %all-gather = f32[512,64]{0,1:T(8,128)S(1)} all-gather(f32[128,64]{0,1:T(8,128)} %param.12), channel_id=2, replica_groups=mesh['space'=8,'shell'=4] {'shell'}, dimensions={0}, use_global_device_ids=true | all-gather | bytes 163840 | tf_op jit(solution)/shard_map/all_gather | solution.py:130
  27.5 1.2 reshape.186
  29.4 2.9 %fusion.37 = f32[4,128,1024]{2,1,0:T(8,128)S(1)} fusion(f32[4,256,128]{1,2,0:T(8,128)} %reshape.186, f32[1024,256,1]{1,0,2:T(8,128)S(1)} %reshape.196), kind=kOutput, calls=%fused_computation.59 | convolution fusion | flops 1610612736 | bytes 3670016 | tf_op jit(solution)/shard_map/rk,qkc->qrc/dot_general | solution.py:160
  32.8 1.8 copy.61
  34.6 5.5 %all-to-all-start.1 = ((f32[32,128,128]{2,1,0:T(8,128)}), f32[32,128,128]{2,1,0:T(8,128)S(1)}, u32[]{:S(2)}, u32[]{:S(2)}) async-start(f32[32,128,128]{2,1,0:T(8,128)} %bitcast.69), calls=%async_computation.1 | async-start | bytes 4194304 | tf_op jit(solution)/shard_map/all_to_all | solution.py:162
  40.1 0.6 multiply_reduce_fusion
  41.2 53.2 %all_gather.9 = s32[4,8,256]{2,1,0:T(8,128)S(1)} all-gather(s32[1,8,256]{2,1,0:T(8,128)S(1)} %bitcast.86), channel_id=1, replica_groups=mesh['space'=8,'shell'=4] {'shell'}, dimensions={0}, use_global_device_ids=true | all-gather | bytes 40960 | tf_op jit(solution)/shard_map/all_gather | solution.py:128
  94.4 0.6 copy.70
  95.0 1.3 neg.6
  96.3 1.9 copy.62
  98.3 3.1 %concatenate.15.start_ref = f32[4096,128]{1,0:T(8,128)} pad(f32[4096,64]{1,0:T(8,128)} %bitcast.71, f32[]{:T(128)} %constant.34.clone.1), padding=0_0x0_64 | pad | bytes 3145732 | tf_op jit(solution)/shard_map/concatenate | solution.py:166
  102.0 0.6 fusion.29.counts_ref
  102.6 1.3 copy-done
  103.9 22.4 %shard_map.86 = (f32[4096,128]{1,0:T(8,128)}, f32[32,2,128]{2,1,0:T(2,128)}) custom-call(s32[8192]{0:T(1024)} %bitcast.77, f32[8192]{0:T(1024)} %bitcast.81, s32[32]{0:T(128)} %fusion.29.counts_ref, f32[4096,128]{1,0:T(8,128)} %bitcast.66, f32[4096,128]{1,0:T(8,128)} %concatenate.15.start_ref), custom_call_target="tpu_custom_call" | custom-call | flops 100000000 | bytes 100000000 | tf_op jit(solution)/shard_map/pallas_call | solution.py:101
  126.3 10.4 %all-to-all-start.2 = ((f32[32,1,256]{2,1,0:T(1,128)}), f32[32,1,256]{2,1,0:T(1,128)S(1)}, u32[]{:S(2)}, u32[]{:S(2)}) async-start(f32[32,1,256]{2,1,0:T(1,128)} %bitcast.88), calls=%async_computation.2 | async-start | bytes 65536 | tf_op jit(solution)/shard_map/all_to_all | solution.py:184
  136.8 1.1 fusion.7
  137.9 6.2 %all-to-all-done.2 = f32[32,1,256]{2,1,0:T(1,128)S(1)} async-done(((f32[32,1,256]{2,1,0:T(1,128)}), f32[32,1,256]{2,1,0:T(1,128)S(1)}, u32[]{:S(2)}, u32[]{:S(2)}) %all-to-all-start.2) | async-done | bytes 32800 | tf_op jit(solution)/shard_map/all_to_all | solution.py:184
  144.2 1.1 fusion.6
  145.3 1.2 fusion.1
  146.6 9.6 %all_to_all.45 = f32[32,1,256]{2,1,0:T(1,128)} all-to-all(f32[32,1,256]{2,1,0:T(1,128)S(1)} %all_to_all.35), channel_id=1, replica_groups=mesh['space'=8,'shell'=4] {'space','shell'}, dimensions={0} | all-to-all | bytes 65536 | tf_op jit(solution)/shard_map/all_to_all | solution.py:176
  156.2 22.4 %shard_map.87 = (f32[4096,128]{1,0:T(8,128)}, f32[32,2,128]{2,1,0:T(2,128)}) custom-call(s32[8192]{0:T(1024)} %bitcast.78, f32[8192]{0:T(1024)} %bitcast.82, s32[32]{0:T(128)} %fusion.29.counts_ref, f32[4096,128]{1,0:T(8,128)} %bitcast.67, f32[4096,128]{1,0:T(8,128)} %concatenate.15.start_ref), custom_call_target="tpu_custom_call" | custom-call | flops 100000000 | bytes 100000000 | tf_op jit(solution)/shard_map/pallas_call | solution.py:101
  178.7 9.1 %all-to-all-start.4 = ((f32[32,1,256]{2,1,0:T(1,128)}), f32[32,1,256]{2,1,0:T(1,128)S(1)}, u32[]{:S(2)}, u32[]{:S(2)}) async-start(f32[32,1,256]{2,1,0:T(1,128)} %bitcast.87), calls=%async_computation.4 | async-start | bytes 65536 | tf_op jit(solution)/shard_map/all_to_all | solution.py:184
  187.8 1.7 slice_bitcast_fusion
  189.5 1.6 copy.65
  191.1 4.0 %all-to-all-done.4 = f32[32,1,256]{2,1,0:T(1,128)S(1)} async-done(((f32[32,1,256]{2,1,0:T(1,128)}), f32[32,1,256]{2,1,0:T(1,128)S(1)}, u32[]{:S(2)}, u32[]{:S(2)}) %all-to-all-start.4) | async-done | bytes 32800 | tf_op jit(solution)/shard_map/all_to_all | solution.py:184
  195.2 1.7 fusion.4
  (40 shorter events, 3.2 us)
Async XLA Ops:
  2.2 26.5 %copy-start.1 = (f32[1,1,8,256,128]{4,3,2,1,0:T(8,128)S(1)}, f32[1,1,8,256,128]{4,3,2,1,0:T(8,128)}, u32[]{:S(2)}) copy-start(f32[1,1,8,256,128]{4,3,2,1,0:T(8,128)} %param.9) | copy-start | bytes 3145732
  5.0 29.6 %all-to-all-start = ((f32[32,1,384]{2,1,0:T(1,128)}), f32[32,1,384]{2,1,0:T(1,128)S(1)}, u32[]{:S(2)}, u32[]{:S(2)}) async-start(f32[32,1,384]{2,1,0:T(1,128)} %all_to_all.39), calls=%async_computation | async-start | bytes 98304 | tf_op jit(solution)/shard_map/all_to_all | solution.py:176
  34.6 6.4 %copy-start.2 = (s32[1,1,8,256]{3,2,1,0:T(8,128)S(1)}, s32[1,1,8,256]{3,2,1,0:T(8,128)}, u32[]{:S(2)}) copy-start(s32[1,1,8,256]{3,2,1,0:T(8,128)} %param.11) | copy-start | bytes 24580
  34.6 68.0 %all-to-all-start.1 = ((f32[32,128,128]{2,1,0:T(8,128)}), f32[32,128,128]{2,1,0:T(8,128)S(1)}, u32[]{:S(2)}, u32[]{:S(2)}) async-start(f32[32,128,128]{2,1,0:T(8,128)} %bitcast.69), calls=%async_computation.1 | async-start | bytes 4194304 | tf_op jit(solution)/shard_map/all_to_all | solution.py:162
  102.6 1.3 copy-start
  103.9 40.3 %copy-start.3 = (f32[2048]{0:T(1024)S(1)}, f32[2048]{0:T(1024)}, u32[]{:S(2)}) copy-start(f32[2048]{0:T(1024)} %param.7) | copy-start | bytes 24580
  126.3 17.7 %all-to-all-start.2 = ((f32[32,1,256]{2,1,0:T(1,128)}), f32[32,1,256]{2,1,0:T(1,128)S(1)}, u32[]{:S(2)}, u32[]{:S(2)}) async-start(f32[32,1,256]{2,1,0:T(1,128)} %bitcast.88), calls=%async_computation.2 | async-start | bytes 65536 | tf_op jit(solution)/shard_map/all_to_all | solution.py:184
  178.7 16.4 %all-to-all-start.4 = ((f32[32,1,256]{2,1,0:T(1,128)}), f32[32,1,256]{2,1,0:T(1,128)S(1)}, u32[]{:S(2)}, u32[]{:S(2)}) async-start(f32[32,1,256]{2,1,0:T(1,128)} %bitcast.87), calls=%async_computation.4 | async-start | bytes 65536 | tf_op jit(solution)/shard_map/all_to_all | solution.py:184

commit v2 on v1

--- a/solution.py
+++ b/solution.py
@@ -10,13 +10,15 @@
 ITERS = 2
 LANES = 128
 ROWS_STEP = 8
+EXTRA = 8
+MESH = pl.DeviceIdType.MESH
 HIGH = lax.Precision.HIGHEST
 
 
 def local_kernel(dirs, voxel_ref, x_ref, counts_ref, pairs_ref, start_ref, resid_ref, grad_ref,
                  even0, odd0, even1, odd1, products):
     blocks = counts_ref.shape[0]
-    rows = pairs_ref.shape[0] // blocks
+    rows = pairs_ref.shape[1] - EXTRA
     even0[...] = start_ref[...]
     odd0[...] = jnp.zeros_like(odd0)
     even1[...] = jnp.zeros_like(even1)
@@ -28,9 +30,8 @@
 
     def scatter_block(block, carry):
         def step(at, carry):
-            base = pl.multiple_of(block * rows + at * ROWS_STEP, ROWS_STEP)
             scal = block * (2 * rows) + at * ROWS_STEP
-            tile = pairs_ref[pl.ds(base, ROWS_STEP), :]
+            tile = pairs_ref[block, pl.ds(pl.multiple_of(at * ROWS_STEP, ROWS_STEP), ROWS_STEP), :]
             for r in range(ROWS_STEP):
                 row = tile[r:r + 1, :]
                 even, odd = (even0, odd0) if r % 2 == 0 else (even1, odd1)
@@ -68,7 +69,8 @@
                     jnp.where(left_row, resid_ref[pl.ds(va, 1), :], resid_ref[pl.ds(vb, 1), :])
                 )
             tile = jnp.concatenate(picked, axis=0)
-            products[pl.ds(base, ROWS_STEP), :] = tile * pairs_ref[pl.ds(base, ROWS_STEP), :]
+            part = pl.ds(pl.multiple_of(at * ROWS_STEP, ROWS_STEP), ROWS_STEP)
+            products[pl.ds(base, ROWS_STEP), :] = tile * pairs_ref[block, part, :]
             return carry
 
         return lax.fori_loop(0, steps_of(block), step, carry)
@@ -85,7 +87,7 @@
             select, part, (((1,), (1,)), ((), ())), precision=HIGH,
             preferred_element_type=jnp.float32,
         )
-        grad_ref[block] = sums[0:2, :]
+        grad_ref[block] = sums
         return carry
 
     lax.fori_loop(0, blocks, reduce_rows, 0)
@@ -93,7 +95,7 @@
 
 def local_step(voxel, x_slots, counts, pairs, start, dirs):
     blocks = counts.shape[0]
-    rows = pairs.shape[0] // blocks
+    rows = pairs.shape[1] - EXTRA
     voxels = start.shape[0]
     vmem = pl.BlockSpec(memory_space=pltpu.VMEM)
     smem = pl.BlockSpec(memory_space=pltpu.SMEM)
@@ -102,17 +104,187 @@
         functools.partial(local_kernel, dirs),
         out_shape=(
             jax.ShapeDtypeStruct((voxels, 2 * dirs), jnp.float32),
-            jax.ShapeDtypeStruct((blocks, 2, rows), jnp.float32),
+            jax.ShapeDtypeStruct((blocks, 8, rows), jnp.float32),
         ),
         in_specs=[smem, smem, smem, vmem, vmem],
         out_specs=(vmem, vmem),
-        scratch_shapes=[wide, wide, wide, wide, pltpu.VMEM(pairs.shape, jnp.float32)],
+        scratch_shapes=[wide, wide, wide, wide, pltpu.VMEM((blocks * rows, 2 * dirs), jnp.float32)],
         compiler_params=pltpu.CompilerParams(vmem_limit_bytes=56 * 1024 * 1024),
         cost_estimate=pl.CostEstimate(flops=10**8, bytes_accessed=10**8, transcendentals=0),
     )(voxel, x_slots, counts, pairs, start)
 
 
-def on_device(shells, weights, seg_streamline, seg_features, pair_counts, seg_voxel, dictionary,
+def greet_all(spaces, shells, me_space, me_shell):
+    total = spaces * shells
+    me = me_space * shells + me_shell
+    barrier = pltpu.get_barrier_semaphore()
+
+    def greet(k, carry):
+        other = lax.rem(me + k, total)
+        pl.semaphore_signal(
+            barrier, inc=1, device_id=(lax.div(other, shells), lax.rem(other, shells)),
+            device_id_type=MESH,
+        )
+        return carry
+
+    lax.fori_loop(1, total, greet, 0)
+    pl.semaphore_wait(barrier, total - 1)
+
+
+def exchange_kernel(spaces, shells, feat_ref, head_ref, small_ref, pairs_ref, heads_ref,
+                    sent, woven, send_sem, recv_sem, head_send, head_recv):
+    me_space, me_shell = lax.axis_index("space"), lax.axis_index("shell")
+    me = me_space * shells + me_shell
+    total = spaces * shells
+    rows = feat_ref.shape[0] // spaces
+    coeffs = feat_ref.shape[1] // 2
+    dirs = sent.shape[2] // 2
+    greet_all(spaces, shells, me_space, me_shell)
+
+    heads_ref[me_shell] = head_ref[...]
+
+    def head_copy(k):
+        other = lax.rem(me_shell + k, shells)
+        return pltpu.make_async_remote_copy(
+            src_ref=head_ref, dst_ref=heads_ref.at[me_shell],
+            send_sem=head_send.at[k], recv_sem=head_recv.at[k],
+            device_id=(me_space, other), device_id_type=MESH,
+        )
+
+    for k in range(1, shells):
+        head_copy(k).start()
+
+    def copy_to(space, shell):
+        at = space * shells + shell
+        return pltpu.make_async_remote_copy(
+            src_ref=sent.at[at], dst_ref=pairs_ref.at[me],
+            send_sem=send_sem.at[at], recv_sem=recv_sem.at[me],
+            device_id=(space, shell), device_id_type=MESH,
+        )
+
+    woven[...] = jnp.zeros_like(woven)
+    for k in range(shells):
+        shell = lax.rem(me_shell + shells - k, shells)
+        if k > 0:
+            head_copy(k).wait_recv()
+        part = heads_ref[shell, 0:dirs, :]
+        woven[0:dirs, 0:coeffs] = part
+        woven[dirs:2 * dirs, coeffs:2 * coeffs] = part
+
+        def send(step, carry):
+            space = lax.rem(me_space + step, spaces)
+            block = feat_ref[pl.ds(pl.multiple_of(space * rows, rows), rows), :]
+            value = lax.dot_general(
+                block, woven[...], (((1,), (1,)), ((), ())), precision=HIGH,
+                preferred_element_type=jnp.float32,
+            )
+            at = space * shells + shell
+            sent[at, 0:rows, :] = value
+            sent[at, rows:rows + EXTRA, :] = small_ref[space]
+            copy_to(space, shell).start()
+            return carry
+
+        if k == 0:
+            value = lax.dot_general(
+                feat_ref[pl.ds(pl.multiple_of(me_space * rows, rows), rows), :], woven[...],
+                (((1,), (1,)), ((), ())), precision=HIGH, preferred_element_type=jnp.float32,
+            )
+            pairs_ref[me, 0:rows, :] = value
+            pairs_ref[me, rows:rows + EXTRA, :] = small_ref[me_space]
+        lax.fori_loop(1 if k == 0 else 0, spaces, send, 0)
+
+    def finish(k, carry):
+        other = lax.rem(me + k, total)
+        space, shell = lax.div(other, shells), lax.rem(other, shells)
+        copy_to(space, shell).wait_send()
+        pltpu.make_async_remote_copy(
+            src_ref=sent.at[other], dst_ref=pairs_ref.at[other],
+            send_sem=send_sem.at[other], recv_sem=recv_sem.at[other],
+            device_id=(space, shell), device_id_type=MESH,
+        ).wait_recv()
+        return carry
+
+    lax.fori_loop(1, total, finish, 0)
+    for k in range(1, shells):
+        head_copy(k).wait_send()
+
+
+def exchange(spaces, shells, feat_pairs, head, small):
+    rows = feat_pairs.shape[0] // spaces
+    dirs = head.shape[0] - 2 * spaces
+    total = spaces * shells
+    vmem = pl.BlockSpec(memory_space=pltpu.VMEM)
+    out = (total, rows + EXTRA, 2 * dirs)
+    return pl.pallas_call(
+        functools.partial(exchange_kernel, spaces, shells),
+        out_shape=(
+            jax.ShapeDtypeStruct(out, jnp.float32),
+            jax.ShapeDtypeStruct((shells,) + head.shape, jnp.float32),
+        ),
+        in_specs=[vmem] * 3,
+        out_specs=(vmem, vmem),
+        scratch_shapes=[
+            pltpu.VMEM(out, jnp.float32),
+            pltpu.VMEM((2 * dirs, feat_pairs.shape[1]), jnp.float32),
+            pltpu.SemaphoreType.DMA((total,)),
+            pltpu.SemaphoreType.DMA((total,)),
+            pltpu.SemaphoreType.DMA((shells,)),
+            pltpu.SemaphoreType.DMA((shells,)),
+        ],
+        compiler_params=pltpu.CompilerParams(
+            collective_id=0, has_side_effects=True, vmem_limit_bytes=56 * 1024 * 1024
+        ),
+    )(feat_pairs, head, small)
+
+
+def message_kernel(spaces, shells, shared, from_ref, to_ref, send_sem, recv_sem):
+    me_space, me_shell = lax.axis_index("space"), lax.axis_index("shell")
+    me = me_space * shells + me_shell
+    total = spaces * shells
+    greet_all(spaces, shells, me_space, me_shell)
+
+    def source(at):
+        return lax.div(at, shells) if shared else at
+
+    def copy_of(other, slot):
+        return pltpu.make_async_remote_copy(
+            src_ref=from_ref.at[source(other)], dst_ref=to_ref.at[slot],
+            send_sem=send_sem.at[other], recv_sem=recv_sem.at[slot],
+            device_id=(lax.div(other, shells), lax.rem(other, shells)), device_id_type=MESH,
+        )
+
+    def send(k, carry):
+        copy_of(lax.rem(me + k, total), me).start()
+        return carry
+
+    lax.fori_loop(1, total, send, 0)
+    to_ref[me] = from_ref[source(me)]
+
+    def finish(k, carry):
+        other = lax.rem(me + k, total)
+        copy_of(other, me).wait_send()
+        copy_of(other, other).wait_recv()
+        return carry
+
+    lax.fori_loop(1, total, finish, 0)
+
+
+def message(spaces, shells, shared, values):
+    total = spaces * shells
+    vmem = pl.BlockSpec(memory_space=pltpu.VMEM)
+    return pl.pallas_call(
+        functools.partial(message_kernel, spaces, shells, shared),
+        out_shape=jax.ShapeDtypeStruct((total,) + values.shape[1:], jnp.float32),
+        in_specs=[vmem],
+        out_specs=vmem,
+        scratch_shapes=[pltpu.SemaphoreType.DMA((total,)), pltpu.SemaphoreType.DMA((total,))],
+        compiler_params=pltpu.CompilerParams(
+            collective_id=2 if shared else 1, has_side_effects=True
+        ),
+    )(values)
+
+
+def on_device(spaces, shells, weights, seg_streamline, seg_features, pair_counts, seg_voxel, dictionary,
               measured):
     blocks = seg_streamline.shape[2]
     slots = seg_streamline.shape[3]
@@ -124,10 +296,9 @@
 
     owner = seg_streamline.reshape(blocks, rows, 2).transpose(0, 2, 1).reshape(-1)
     voxel = seg_voxel.reshape(blocks, rows, 2).transpose(0, 2, 1).reshape(blocks, slots)
-    voxel_all = (
-        lax.all_gather(voxel, "shell", axis=0).transpose(1, 0, 2).reshape(blocks * shells * slots)
+    head = jnp.concatenate(
+        [dictionary.T, voxel.reshape(2 * blocks, rows).astype(jnp.float32)], axis=0
     )
-    dict_all = lax.all_gather(dictionary, "shell", axis=0)
 
     live = lax.broadcasted_iota(jnp.int32, (blocks, slots), 1) < counts[:, None]
     masked = jnp.where(
@@ -152,40 +323,25 @@
 
     scaling = 0.5 / (0.5 + add_up(sq))
 
-    zero = jnp.zeros_like(dict_all)
-    weave = jnp.stack(
-        [jnp.concatenate([dict_all, zero], axis=2), jnp.concatenate([zero, dict_all], axis=2)],
-        axis=1,
-    ).reshape(shells, 2 * coeffs, 2 * dirs)
-    projected = jnp.einsum("rk,qkc->qrc", feat_pairs, weave, precision=HIGH)
-    projected = projected.reshape(shells, blocks, rows, 2 * dirs).transpose(1, 0, 2, 3)
-    pairs = lax.all_to_all(
-        projected.reshape(blocks * shells, rows, 2 * dirs), ("space", "shell"), 0, 0, tiled=True
-    ).reshape(blocks * shells * rows, 2 * dirs)
+    current = weights.reshape(streams // LANES, LANES)
+    extra = jnp.broadcast_to(counts[:, None, None].astype(jnp.float32), (blocks, EXTRA - 2, rows))
+    small = jnp.concatenate([pick(current).reshape(blocks, 2, rows), extra], axis=1)
+    pairs, heads = exchange(spaces, shells, feat_pairs, head, small)
+    voxel_all = heads[:, dirs:, :].astype(jnp.int32).reshape(shells, blocks, slots)
+    voxel_all = voxel_all.transpose(1, 0, 2).reshape(-1)
+    x_slots = pairs[:, rows:rows + 2, :].reshape(-1)
+    counts_all = pairs[:, rows + 2, 0].astype(jnp.int32)
 
     start = jnp.concatenate([-measured.T, jnp.zeros_like(measured).T], axis=1)
 
-    current = weights.reshape(streams // LANES, LANES)
-    counts_all = None
     for iteration in range(ITERS):
-        sent = pick(current).reshape(blocks, slots)
-        if iteration == 0:
-            extra = jnp.broadcast_to(counts[:, None].astype(jnp.float32), (blocks, LANES))
-            sent = jnp.concatenate([sent, extra], axis=1)
-        sent = jnp.broadcast_to(sent[:, None, :], (blocks, shells, sent.shape[1]))
-        got = lax.all_to_all(
-            sent.reshape(blocks * shells, -1), ("space", "shell"), 0, 0, tiled=True
-        )
-        if iteration == 0:
-            counts_all = got[:, slots].astype(jnp.int32)
-        resid, grads = local_step(
-            voxel_all, got[:, :slots].reshape(-1), counts_all, pairs, start, dirs
-        )
-        back = lax.all_to_all(
-            grads.reshape(blocks * shells, slots), ("space", "shell"), 0, 0, tiled=True
-        )
-        slot_grad = jnp.sum(back.reshape(blocks, shells, slots), axis=1)
+        resid, grads = local_step(voxel_all, x_slots, counts_all, pairs, start, dirs)
+        back = message(spaces, shells, False, grads)
+        slot_grad = jnp.sum(back.reshape(blocks, shells, 8, rows)[:, :, 0:2], axis=1)
         current = jnp.maximum(current - scaling * add_up(slot_grad.reshape(-1)), 0.0)
+        if iteration < ITERS - 1:
+            sent = jnp.pad(pick(current).reshape(blocks, 2, rows), ((0, 0), (0, 6), (0, 0)))
+            x_slots = message(spaces, shells, True, sent)[:, 0:2, :].reshape(-1)
     return current.reshape(streams), resid[:, :dirs].T
 
 
@@ -201,6 +357,6 @@
     )
     out_specs = (P(("space", "shell")), P("shell", "space"))
     return jax.shard_map(
-        functools.partial(on_device, mesh.shape["shell"]),
+        functools.partial(on_device, mesh.shape["space"], mesh.shape["shell"]),
         mesh=mesh, in_specs=in_specs, out_specs=out_specs, check_vma=False,
     )

time: 196 us -> 187 us (0.954); the launches traced: 197 us -> 185 us
  Pallas kernels: 44.9 us -> 154 us
  blocking collectives: 76.7 us -> 0 us
  starting transfers between devices: 32.3 us -> 0 us
  waiting for transfers between devices: 10.2 us -> 0 us
  other arithmetic: 5.01 us -> 11.9 us
  local copies, waits for them, and re-layouts: 16.9 us -> 12 us
  matrix products: 10 us -> 6.33 us
    pallas_call x0 -> x4, Pallas kernels: none -> 108 us  [the longest x1 62.6 us: exchange(): pl.pallas_call(functools.partial(exchange_kernel, spaces, shells), out_sh...]
    all_gather x2 -> x0, blocking collectives: 67.1 us -> none  [the longest x1 53.2 us: on_device(): lax.all_gather(voxel, 'shell', axis=0).transpose(1, 0, 2)]
    all_to_all x4 -> x0, starting transfers between devices: 32.3 us -> none  [the longest x2 19.5 us: on_device(): lax.all_to_all(grads.reshape(blocks * shells, slots), ('space', 'shell'),...]
    all_to_all x4 -> x0, waiting for transfers between devices: 10.2 us -> none  [the longest x2 10.2 us: on_device(): lax.all_to_all(grads.reshape(blocks * shells, slots), ('space', 'shell'),...]
    all_to_all x1 -> x0, blocking collectives: 9.61 us -> none  [on_device(): lax.all_to_all(sent.reshape(blocks * shells, -1), ('space', 'shell'), 0,...]
    slice x0 -> x2, local copies, waits for them, and re-layouts: none -> 3.04 us  [the longest x1 1.52 us: on_device(): x_slots = message(spaces, shells, True, sent)[:, 0:2, :].reshape(-1)]
    convert_element_type x2 -> x4, other arithmetic: 1.29 us -> 4.22 us  [the longest x1 2.08 us: on_device(): counts_all = pairs[:, rows + 2, 0].astype(jnp.int32)]
    dot_general x1 -> x0, matrix products: 2.91 us -> none  [on_device(): projected = jnp.einsum('rk,qkc->qrc', feat_pairs, weave, precision=HIGH)]
  transfers between devices with their start and end apart: 4 -> 0, of which waited for: 2 -> 0; matrix products, arithmetic and copies ran while one was open for 11% -> 0% of each run, Pallas kernels for 0% -> 0%
where the time goes in v2:
time: 187 us; the launch traced here: 185 us
  Pallas kernels  154 us (82%)
  local copies, waits for them, and re-layouts  12 us (6%)
  other arithmetic  11.9 us (6%)
  matrix products  6.33 us (3%)
    pallas_call x1, Pallas kernels, exchange(): pl.pallas_call(functools.partial(exchange_kernel, spaces, shells), out_sh...  62.6 us
    pallas_call x2, Pallas kernels, local_step(): pl.pallas_call(functools.partial(local_kernel, dirs), out_shape=(jax.Shap...  46.7 us
    pallas_call x3, Pallas kernels, message(): pl.pallas_call(functools.partial(message_kernel, spaces, shells, shared),...  45 us
    dot_general x3, matrix products, add_up(): lax.dot_general(hi, jnp.where(lo, values[:, None], 0.0), (((0,), (0,)), (...  3.93 us

profile of v2, /device:TPU:0, one launch (start us, length us, event | category | flops | bytes accessed | tf_op | source)
XLA Modules:
  0.0 185.4 jit_solution(8524707207581454189)
XLA Ops:
  0.6 0.7 bitcast_convert_fusion
  1.3 0.7 iota_compare_fusion.7
  2.0 1.9 %multiply_reduce_fusion = f32[8,256]{1,0:T(8,128)S(1)} fusion(f32[1,1,8,256,128]{4,3,2,1,0:T(8,128)} %param.9, pred[8,256]{1,0:T(8,128)(4,1)S(1)} %iota_compare_fusion.7), kind=kLoop, calls=%fused_computation.17 | loop fusion | flops 784384 | bytes 1058816 | tf_op jit(solution)/shard_map/reduce_sum | solution.py:308
  3.9 0.7 convert_element_type.31
  4.9 1.4 pad_maximum_fusion.head_ref
  6.5 0.8 copy.29
  7.4 1.1 fusion.7
  8.6 1.2 fusion
  9.8 0.6 pad_maximum_fusion.1.small_ref
  10.4 0.3 broadcast_in_dim.64
  11.0 0.6 copy.36
  11.7 1.4 concatenate.11.start_ref
  13.6 1.1 broadcast_select_fusion.feat_ref
  14.6 62.6 %shard_map.86 = (f32[32,136,128]{2,1,0:T(8,128)}, f32[4,80,128]{2,1,0:T(8,128)}) custom-call(f32[1024,256]{1,0:T(8,128)} %broadcast_select_fusion.feat_ref, f32[80,128]{1,0:T(8,128)} %pad_maximum_fusion.head_ref, f32[8,8,128]{2,1,0:T(8,128)} %pad_maximum_fusion.1.small_ref), custom_call_target="tpu_custom_call" | custom-call | tf_op jit(solution)/shard_map/pallas_call | solution.py:218
  77.3 0.8 slice_convert_fusion
  78.1 0.6 copy.38
  78.7 2.1 %convert_reduce_fusion.counts_ref = s32[32]{0:T(128)} fusion(f32[32,136,128]{2,1,0:T(8,128)} %get-tuple-element.8.pairs_ref), kind=kLoop, calls=%fused_computation.42 | loop fusion | flops 32 | bytes 256 | tf_op jit(solution)/shard_map/convert_element_type | solution.py:333
  80.8 1.5 slice.22
  82.3 23.4 %shard_map.87 = (f32[4096,128]{1,0:T(8,128)}, f32[32,8,128]{2,1,0:T(8,128)}) custom-call(s32[8192]{0:T(1024)} %bitcast.44, f32[8192]{0:T(1024)} %bitcast.49, s32[32]{0:T(128)} %convert_reduce_fusion.counts_ref, f32[32,136,128]{2,1,0:T(8,128)} %get-tuple-element.8.pairs_ref, f32[4096,128]{1,0:T(8,128)} %concatenate.11.start_ref), custom_call_target="tpu_custom_call" | custom-call | flops 100000000 | bytes 100000000 | tf_op jit(solution)/shard_map/pallas_call | solution.py:103
  105.7 17.4 %shard_map.88 = f32[32,8,128]{2,1,0:T(8,128)} custom-call(f32[32,8,128]{2,1,0:T(8,128)} %get-tuple-element.9.from_ref), custom_call_target="tpu_custom_call" | custom-call | tf_op jit(solution)/shard_map/pallas_call | solution.py:275
  123.0 0.9 slice_reduce_fusion.1
  124.0 1.1 fusion.6
  125.1 1.2 fusion.1
  126.3 0.6 pad.5.from_ref
  126.9 10.8 %shard_map.89 = f32[32,8,128]{2,1,0:T(8,128)} custom-call(f32[8,8,128]{2,1,0:T(8,128)} %pad.5.from_ref), custom_call_target="tpu_custom_call" | custom-call | tf_op jit(solution)/shard_map/pallas_call | solution.py:275
  137.7 1.5 slice.25
  139.2 23.4 %shard_map.90 = (f32[4096,128]{1,0:T(8,128)}, f32[32,8,128]{2,1,0:T(8,128)}) custom-call(s32[8192]{0:T(1024)} %bitcast.45, f32[8192]{0:T(1024)} %bitcast.48, s32[32]{0:T(128)} %convert_reduce_fusion.counts_ref, f32[32,136,128]{2,1,0:T(8,128)} %get-tuple-element.8.pairs_ref, f32[4096,128]{1,0:T(8,128)} %concatenate.11.start_ref), custom_call_target="tpu_custom_call" | custom-call | flops 100000000 | bytes 100000000 | tf_op jit(solution)/shard_map/pallas_call | solution.py:103
  162.6 16.9 %shard_map.91 = f32[32,8,128]{2,1,0:T(8,128)} custom-call(f32[32,8,128]{2,1,0:T(8,128)} %get-tuple-element.10.from_ref), custom_call_target="tpu_custom_call" | custom-call | tf_op jit(solution)/shard_map/pallas_call | solution.py:275
  179.5 0.9 slice_reduce_fusion
  180.4 1.7 fusion.4
  182.1 1.7 slice_bitcast_fusion
  183.9 1.6 copy.37
  (18 shorter events, 1.3 us)
Async XLA Ops:
  0.6 7.9 %copy-start.2 = (f32[2048]{0:T(1024)S(1)}, f32[2048]{0:T(1024)}, u32[]{:S(2)}) copy-start(f32[2048]{0:T(1024)} %param.7) | copy-start | bytes 24580
  4.6 6.3 %copy-start.1 = (f32[64,4096]{1,0:T(8,128)S(1)}, f32[64,4096]{1,0:T(8,128)}, u32[]{:S(2)}) copy-start(f32[64,4096]{1,0:T(8,128)} %param.13) | copy-start | bytes 3145732
  11.6 1.6 copy-start

commit v3 on v2

--- a/solution.py
+++ b/solution.py
@@ -37,8 +37,8 @@
                 even, odd = (even0, odd0) if r % 2 == 0 else (even1, odd1)
                 va = voxel_ref[scal + r]
                 vb = voxel_ref[scal + rows + r]
-                even[pl.ds(va, 1), :] = even[pl.ds(va, 1), :] + x_ref[scal + r] * row
-                odd[pl.ds(vb, 1), :] = odd[pl.ds(vb, 1), :] + x_ref[scal + rows + r] * row
+                even[pl.ds(va, 1), :] = even[pl.ds(va, 1), :] + x_ref[block, 0, at * ROWS_STEP + r] * row
+                odd[pl.ds(vb, 1), :] = odd[pl.ds(vb, 1), :] + x_ref[block, 1, at * ROWS_STEP + r] * row
             return carry
 
         return lax.fori_loop(0, steps_of(block), step, carry)
@@ -87,7 +87,7 @@
             select, part, (((1,), (1,)), ((), ())), precision=HIGH,
             preferred_element_type=jnp.float32,
         )
-        grad_ref[block] = sums
+        grad_ref[block] = sums[0:2, :]
         return carry
 
     lax.fori_loop(0, blocks, reduce_rows, 0)
@@ -104,7 +104,7 @@
         functools.partial(local_kernel, dirs),
         out_shape=(
             jax.ShapeDtypeStruct((voxels, 2 * dirs), jnp.float32),
-            jax.ShapeDtypeStruct((blocks, 8, rows), jnp.float32),
+            jax.ShapeDtypeStruct((blocks, 2, rows), jnp.float32),
         ),
         in_specs=[smem, smem, smem, vmem, vmem],
         out_specs=(vmem, vmem),
@@ -329,7 +329,7 @@
     pairs, heads = exchange(spaces, shells, feat_pairs, head, small)
     voxel_all = heads[:, dirs:, :].astype(jnp.int32).reshape(shells, blocks, slots)
     voxel_all = voxel_all.transpose(1, 0, 2).reshape(-1)
-    x_slots = pairs[:, rows:rows + 2, :].reshape(-1)
+    x_slots = pairs[:, rows:rows + 2, :]
     counts_all = pairs[:, rows + 2, 0].astype(jnp.int32)
 
     start = jnp.concatenate([-measured.T, jnp.zeros_like(measured).T], axis=1)
@@ -337,11 +337,10 @@
     for iteration in range(ITERS):
         resid, grads = local_step(voxel_all, x_slots, counts_all, pairs, start, dirs)
         back = message(spaces, shells, False, grads)
-        slot_grad = jnp.sum(back.reshape(blocks, shells, 8, rows)[:, :, 0:2], axis=1)
+        slot_grad = jnp.sum(back.reshape(blocks, shells, 2, rows), axis=1)
         current = jnp.maximum(current - scaling * add_up(slot_grad.reshape(-1)), 0.0)
         if iteration < ITERS - 1:
-            sent = jnp.pad(pick(current).reshape(blocks, 2, rows), ((0, 0), (0, 6), (0, 0)))
-            x_slots = message(spaces, shells, True, sent)[:, 0:2, :].reshape(-1)
+            x_slots = message(spaces, shells, True, pick(current).reshape(blocks, 2, rows))
     return current.reshape(streams), resid[:, :dirs].T
 
 

time: 187 us -> 194 us (1.037)
  Pallas kernels: 154 us -> 163 us
  local copies, waits for them, and re-layouts: 12 us -> 9.86 us
    pallas_call x3, Pallas kernels: 45 us -> 50.9 us  [message(): pl.pallas_call(functools.partial(message_kernel, spaces, shells, shared),...]
    pallas_call x2, Pallas kernels: 46.7 us -> 49.7 us  [local_step(): pl.pallas_call(functools.partial(local_kernel, dirs), out_shape=(jax.Shap...]
where the time goes in v3:
time: 194 us; the launch traced here: 193 us
  Pallas kernels  163 us (84%)
  other arithmetic  11.7 us (6%)
  local copies, waits for them, and re-layouts  9.86 us (5%)
  matrix products  6.93 us (4%)
    pallas_call x1, Pallas kernels, exchange(): pl.pallas_call(functools.partial(exchange_kernel, spaces, shells), out_sh...  62.6 us
    pallas_call x3, Pallas kernels, message(): pl.pallas_call(functools.partial(message_kernel, spaces, shells, shared),...  50.9 us
    pallas_call x2, Pallas kernels, local_step(): pl.pallas_call(functools.partial(local_kernel, dirs), out_shape=(jax.Shap...  49.7 us
    dot_general x3, matrix products, add_up(): lax.dot_general(hi, jnp.where(lo, values[:, None], 0.0), (((0,), (0,)), (...  3.93 us

profile of v3, /device:TPU:0, one launch (start us, length us, event | category | flops | bytes accessed | tf_op | source)
XLA Modules:
  0.0 192.6 jit_solution(8820556604892022680)
XLA Ops:
  0.6 0.7 bitcast_convert_fusion
  1.3 0.7 iota_compare_fusion.7
  2.0 1.9 multiply_reduce_fusion
  3.9 0.7 convert_element_type.29
  4.9 1.4 pad_maximum_fusion.head_ref
  6.5 0.8 copy.29
  7.4 1.1 fusion.7
  8.6 1.2 fusion
  9.8 0.6 pad_maximum_fusion.1.small_ref
  10.4 0.3 broadcast_in_dim.64
  10.7 0.2 broadcast_in_dim.65
  11.0 0.6 copy.36
  11.7 1.4 concatenate.11.start_ref
  13.3 0.3 reshape.135
  13.6 1.1 broadcast_select_fusion.feat_ref
  14.6 62.6 %shard_map.86 = (f32[32,136,128]{2,1,0:T(8,128)}, f32[4,80,128]{2,1,0:T(8,128)}) custom-call(f32[1024,256]{1,0:T(8,128)} %broadcast_select_fusion.feat_ref, f32[80,128]{1,0:T(8,128)} %pad_maximum_fusion.head_ref, f32[8,8,128]{2,1,0:T(8,128)} %pad_maximum_fusion.1.small_ref), custom_call_target="tpu_custom_call" | custom-call | tf_op jit(solution)/shard_map/pallas_call | solution.py:218
  77.3 0.8 slice_convert_fusion
  78.1 0.6 copy.38
  78.7 2.1 %convert_reduce_fusion.counts_ref = s32[32]{0:T(128)} fusion(f32[32,136,128]{2,1,0:T(8,128)} %get-tuple-element.8.pairs_ref), kind=kLoop, calls=%fused_computation.42 | loop fusion | flops 32 | bytes 256 | tf_op jit(solution)/shard_map/convert_element_type | solution.py:333
  80.9 1.5 slice.13.x_ref
  82.4 24.9 %shard_map.87 = (f32[4096,128]{1,0:T(8,128)}, f32[32,2,128]{2,1,0:T(2,128)}) custom-call(s32[8192]{0:T(1024)} %bitcast.44, f32[32,2,128]{2,1,0:T(2,128)} %slice.13.x_ref, s32[32]{0:T(128)} %convert_reduce_fusion.counts_ref, f32[32,136,128]{2,1,0:T(8,128)} %get-tuple-element.8.pairs_ref, f32[4096,128]{1,0:T(8,128)} %concatenate.11.start_ref), custom_call_target="tpu_custom_call" | custom-call | flops 100000000 | bytes 100000000 | tf_op jit(solution)/shard_map/pallas_call | solution.py:103
  107.3 20.7 %shard_map.88 = f32[32,2,128]{2,1,0:T(2,128)} custom-call(f32[32,2,128]{2,1,0:T(2,128)} %get-tuple-element.9.from_ref), custom_call_target="tpu_custom_call" | custom-call | tf_op jit(solution)/shard_map/pallas_call | solution.py:275
  128.0 0.8 bitcast_reduce_fusion.1
  128.8 1.1 fusion.6
  129.9 1.8 fusion.1
  131.7 9.4 %shard_map.89.x_ref = f32[32,2,128]{2,1,0:T(2,128)} custom-call(f32[8,2,128]{2,1,0:T(2,128)} %bitcast.54), custom_call_target="tpu_custom_call" | custom-call | tf_op jit(solution)/shard_map/pallas_call | solution.py:275
  141.0 24.9 %shard_map.90 = (f32[4096,128]{1,0:T(8,128)}, f32[32,2,128]{2,1,0:T(2,128)}) custom-call(s32[8192]{0:T(1024)} %bitcast.45, f32[32,2,128]{2,1,0:T(2,128)} %shard_map.89.x_ref, s32[32]{0:T(128)} %convert_reduce_fusion.counts_ref, f32[32,136,128]{2,1,0:T(8,128)} %get-tuple-element.8.pairs_ref, f32[4096,128]{1,0:T(8,128)} %concatenate.11.start_ref), custom_call_target="tpu_custom_call" | custom-call | flops 100000000 | bytes 100000000 | tf_op jit(solution)/shard_map/pallas_call | solution.py:103
  165.9 20.8 %shard_map.91 = f32[32,2,128]{2,1,0:T(2,128)} custom-call(f32[32,2,128]{2,1,0:T(2,128)} %get-tuple-element.10.from_ref), custom_call_target="tpu_custom_call" | custom-call | tf_op jit(solution)/shard_map/pallas_call | solution.py:275
  186.8 0.8 bitcast_reduce_fusion
  187.5 1.7 fusion.4
  189.3 1.7 slice_bitcast_fusion
  191.0 1.6 copy.37
  (16 shorter events, 0.8 us)
Async XLA Ops:
  0.6 7.9 %copy-start.2 = (f32[2048]{0:T(1024)S(1)}, f32[2048]{0:T(1024)}, u32[]{:S(2)}) copy-start(f32[2048]{0:T(1024)} %param.7) | copy-start | bytes 24580
  4.6 6.3 %copy-start.1 = (f32[64,4096]{1,0:T(8,128)S(1)}, f32[64,4096]{1,0:T(8,128)}, u32[]{:S(2)}) copy-start(f32[64,4096]{1,0:T(8,128)} %param.13) | copy-start | bytes 3145732
  11.6 1.6 copy-start
